TPU v7x, 256 devices: a whole 4x4x8 slice. The times are simulated.
256 devices in a mesh: tg: 4 (over x), tc: 32 (over z, y), sp: 2 (over core).
Axes of the slice: x: 4, y: 4, z: 8, core: 2. Of those that a mesh axis runs over, the one named last changes fastest.
Arguments:
- initial: float32 [512, 128], P('sp'), may hold values from 0.5 to 1.5
- source: float32 [128, 512, 128], P(('tg', 'tc'), 'sp'), may hold values from -0.3 to 0.3
Outputs:
- c_values: float32 [128, 512, 128], P(('tg', 'tc'), 'sp')
- block_mean: float32 [128, 512, 128], P(('tg', 'tc'), 'sp')
All inputs are finite; a program needn't handle non-finite values.
Results may differ from a plain program's by a relative error of at most 0.00002.
Values sent between devices are 32-bit elements; how exact they have to be, the bound alone decides.
No kernel may reach another device: no remote copies, remote signals or barrier semaphores. Data moves between devices by JAX's collectives and lax.ppermute only.
A program may use at most 128 MiB of HBM per device.

v0:
```python
import jax
import jax.numpy as jnp
from jax import lax
from jax.sharding import PartitionSpec as P

STEPS = 16


fine_center = 0.2
fine_behind = 0.25
fine_ahead = 0.15
coarse_center = 0.04
coarse_behind = 0.31
coarse_ahead = 0.17


def with_halo(block, sides, width):
    for axis, dim in sides:
        count = lax.axis_size(axis)
        forward = [(i, i + 1) for i in range(count - 1)]
        forward.append((count - 1, 0))
        backward = [(target, source) for source, target in forward]
        low = lax.ppermute(
            lax.slice_in_dim(block, block.shape[dim] - width, None, axis=dim), axis, forward
        )
        high = lax.ppermute(lax.slice_in_dim(block, 0, width, axis=dim), axis, backward)
        block = jnp.concatenate([low, block, high], axis=dim)
    return block


def from_behind(block, axis, distance):
    devices = range(lax.axis_size(axis))
    route = [(i - distance, i) for i in devices if i - distance in devices]
    return lax.ppermute(block, axis, route)


def carried_in(part, axis, combine, identity):
    place = lax.axis_index(axis)
    gathered = jax.tree.map(lambda a: lax.all_gather(a, axis), part)
    state = jax.tree.map(lambda a, e: jnp.zeros_like(a) + jnp.asarray(e, a.dtype), part, identity)

    def one(hop, state):
        return combine(
            state, jax.tree.map(lambda a: lax.dynamic_index_in_dim(a, hop, 0, False), gathered)
        )

    return lax.fori_loop(0, place, one, state)


def fine_update(padded, forcing):
    middle = padded[1:-1]
    upper_rows = padded[:-2]
    lower_rows = padded[2:]
    return (
        fine_center * middle
        + fine_behind * upper_rows
        + fine_ahead * lower_rows
        + fine_behind * jnp.roll(middle, 1, 1)
        + fine_ahead * jnp.roll(middle, -1, 1)
        + forcing
    )


def coarse_apply(state):
    return (
        coarse_center * state
        + coarse_behind * jnp.roll(state, 1, 0)
        + coarse_ahead * jnp.roll(state, -1, 0)
        + coarse_behind * jnp.roll(state, 1, 1)
        + coarse_ahead * jnp.roll(state, -1, 1)
    )


def chain_combine(earlier, later):
    earlier_count, earlier_error = earlier
    later_count, later_error = later

    def repeat(step_index, current):
        return coarse_apply(current)

    carried = lax.fori_loop(0, later_count.astype(jnp.int32), repeat, earlier_error)
    return (earlier_count + later_count, carried + later_error)


def march_block(state, forcing, step_count, keep):
    running = jnp.zeros_like(state)
    for step_index in range(step_count):
        padded = with_halo(state, (("sp", 0),), 1)
        state = fine_update(padded, forcing)
        if keep:
            running = running + state
    return (state, running)


def shards(initial, source):
    forcing = source[0]
    slab_rows = forcing.shape[0]
    block_index = lax.axis_index(("tg", "tc"))
    is_first = block_index == 0
    first_start = jnp.zeros_like(initial)
    c_guess, unused_sum = march_block(first_start, forcing, STEPS, False)
    received = from_behind(c_guess, ("tg", "tc"), 1)
    c_start = jnp.where(is_first, initial, received)
    marched, unused_sum = march_block(c_start, forcing, STEPS, False)
    defect = marched - c_guess
    full_defect = lax.all_gather(defect, "sp", axis=0, tiled=True)
    identity = (jnp.zeros((), jnp.float32), jnp.zeros_like(full_defect))
    prefix_count, carried = carried_in(
        (jnp.ones((), jnp.float32), full_defect), ("tg", "tc"), chain_combine, identity
    )
    error_next = coarse_apply(carried) + full_defect
    row_offset = lax.axis_index("sp") * slab_rows
    own_rows = lax.dynamic_slice_in_dim(error_next, row_offset, slab_rows, 0)
    c_values = c_guess + own_rows
    passed = from_behind(c_values, ("tg", "tc"), 1)
    restart = jnp.where(is_first, initial, passed)
    final_state, running = march_block(restart, forcing, STEPS - 1, True)
    block_mean = running / (STEPS - 1)
    return (c_values[None], block_mean[None])


def solution(mesh):
    in_specs = (P("sp", None), P(("tg", "tc"), "sp", None))
    out_specs = (P(("tg", "tc"), "sp", None), P(("tg", "tc"), "sp", None))
    return jax.shard_map(shards, mesh=mesh, in_specs=in_specs, out_specs=out_specs, check_vma=False)
```

profile of v0, /device:TPU:255, one launch (start us, length us, event | category | flops | bytes accessed | tf_op | source)
XLA Modules:
  0.0 849.7 jit_solution(11752303097845805850)
XLA Ops:
  11.6 1.0 fusion.346
  14.2 1.0 fusion.339
  16.8 1.0 fusion.332
  19.5 1.0 fusion.325
  22.1 1.0 fusion.318
  24.7 1.0 fusion.311
  27.3 1.0 fusion.304
  30.0 1.0 fusion.297
  32.8 1.0 fusion.290
  35.4 1.0 fusion.283
  38.0 1.0 fusion.276
  40.7 1.0 fusion.269
  43.3 1.0 fusion.262
  45.9 1.0 fusion.255
  48.5 1.0 fusion.248
  49.6 1.3 collective-permute-start.32
  50.9 5.4 collective-permute-done.32
  56.4 1.2 collective-permute-start.33
  58.7 1.0 fusion.241
  61.3 1.0 fusion.234
  87.1 2.1 all_gather.13
  90.7 289.4 %all-reduce.3 = f32[128]{0:T(128)S(1)} all-reduce(f32[128]{0:T(128)S(1)} %dynamic-update-slice), channel_id=1, replica_groups=mesh['tg'=4,'tc'=32,'sp'=2] {'tg','tc'}, use_global_device_ids=true, to_apply=%add.3 | all-reduce | flops 128 | bytes 1024
  380.1 373.3 %while.26 = (s32[]{:T(128)}, f32[512,128]{1,0:T(8,128)S(1)}, s32[]{:T(128)}, f32[128]{0:T(128)S(1)}, f32[128,512,128]{2,1,0:T(8,128)}, /*index=5*/s32[]{:T(128)}, s32[]{:T(128)}, s32[]{:T(128)}, s32[]{:T(128)}) while((s32[]{:T(128)}, f32[512,128]{1,0:T(8,128)S(1)}, s32[]{:T(128)}, f32[128]{0:T(128)S(1)}, f32[128,512,128]{2,1,0:T(8,128)}, ...), condition=%wide.region_3.4_spmd, body=%wide.region_0.3_spmd.sunk | while | flops 917512 | bytes 4456700 | solution.py:47
  385.0 1.0 bitcast_add_fusion.2
  387.9 1.0 bitcast_add_fusion.2
  396.8 1.0 bitcast_add_fusion.2
  399.7 1.0 bitcast_add_fusion.2
  405.6 1.0 bitcast_add_fusion.2
  408.5 1.0 bitcast_add_fusion.2
  414.4 1.0 bitcast_add_fusion.2
  417.3 1.0 bitcast_add_fusion.2
  423.2 1.0 bitcast_add_fusion.2
  426.2 1.0 bitcast_add_fusion.2
  432.0 1.0 bitcast_add_fusion.2
  435.0 1.0 bitcast_add_fusion.2
  440.9 1.0 bitcast_add_fusion.2
  443.8 1.0 bitcast_add_fusion.2
  452.6 1.0 bitcast_add_fusion.2
  455.6 1.0 bitcast_add_fusion.2
  461.4 1.0 bitcast_add_fusion.2
  464.4 1.0 bitcast_add_fusion.2
  470.3 1.0 bitcast_add_fusion.2
  473.2 1.0 bitcast_add_fusion.2
  479.1 1.0 bitcast_add_fusion.2
  482.0 1.0 bitcast_add_fusion.2
  754.0 1.3 collective-permute-start.65
  755.3 4.4 collective-permute-done.65
  759.9 56.0 %collective-permute-start.66 = (f32[1,128]{1,0:T(1,128)S(1)}, f32[1,128]{1,0:T(1,128)S(1)}, u32[]{:S(2)}, u32[]{:S(2)}) collective-permute-start(f32[1,128]{1,0:T(1,128)S(1)} %get-tuple-element.185), channel_id=1, source_target_pairs={{0,1},{1,0},{2,3},{3,2},{4,5},{5,4},{6,7},{7,6},{8,9},{9,8},{10,11... | collective-permute-start | bytes 1544 | tf_op jit(solution)/shard_map/ppermute | solution.py:23
  (1375 shorter events, 420.7 us)
Async XLA Ops:
  7.2 372.9 %all-gather.3.cloned.1.call-start = ((), (), s32[]{:S(2)}) async-start(), calls=%async_computation | async-start | bytes 33816576 | tf_op jit(solution)/shard_map/all_gather | solution.py:39
  7.2 1.6 collective-permute-start.1
  10.2 1.2 collective-permute-start.2
  12.7 1.2 collective-permute-start.4
  15.4 1.2 collective-permute-start.6
  18.0 1.2 collective-permute-start.8
  20.7 1.2 collective-permute-start.10
  23.2 1.2 collective-permute-start.12
  28.5 1.2 collective-permute-start.16
  31.2 1.4 collective-permute-start.18
  33.9 1.2 collective-permute-start.20
  36.6 1.2 collective-permute-start.22
  39.2 1.2 collective-permute-start.24
  41.8 1.2 collective-permute-start.26
  44.4 1.2 collective-permute-start.28
  49.6 6.7 collective-permute-start.32
  56.4 2.0 collective-permute-start.33
  59.9 1.2 collective-permute-start.35
  62.4 1.6 collective-permute-start.37
  64.6 1.2 collective-permute-start.39
  66.3 1.2 collective-permute-start.41
  68.1 1.2 collective-permute-start.43
  69.8 1.2 collective-permute-start.45
  71.5 1.2 collective-permute-start.47
  73.2 1.2 collective-permute-start.49
  76.7 1.2 collective-permute-start.53
  78.4 1.2 collective-permute-start.55
  78.7 1.3 collective-permute-start.56
  80.3 1.2 collective-permute-start.57
  83.8 1.2 collective-permute-start.61
  85.6 1.2 collective-permute-start.63
  754.0 5.7 collective-permute-start.65
  759.9 56.8 %collective-permute-start.66 = (f32[1,128]{1,0:T(1,128)S(1)}, f32[1,128]{1,0:T(1,128)S(1)}, u32[]{:S(2)}, u32[]{:S(2)}) collective-permute-start(f32[1,128]{1,0:T(1,128)S(1)} %get-tuple-element.185), channel_id=1, source_target_pairs={{0,1},{1,0},{2,3},{3,2},{4,5},{5,4},{6,7},{7,6},{8,9},{9,8},{10,11... | collective-permute-start | bytes 1544 | tf_op jit(solution)/shard_map/ppermute | solution.py:23
  817.2 1.2 collective-permute-start.68
  818.9 1.2 collective-permute-start.70
  820.7 1.2 collective-permute-start.72
  821.0 1.4 collective-permute-start.73
  822.6 1.2 collective-permute-start.74
  824.4 1.2 collective-permute-start.76
  826.1 1.2 collective-permute-start.78
  827.8 1.2 collective-permute-start.80
  829.5 1.2 collective-permute-start.82
  833.0 1.2 collective-permute-start.86
  834.7 1.2 collective-permute-start.88
  836.4 1.2 collective-permute-start.90
  836.8 1.4 collective-permute-start.91
  838.4 1.2 collective-permute-start.92
  840.1 1.2 collective-permute-start.94
  (54 other events, 1036.4 us)
Sparse Core Ops, SparseCore 0:
  89.4 207.8 all-gather.2
where the time goes:
time: 864 us; the launch traced here: 850 us
  blocking collectives  292 us (34%)
  other arithmetic  185 us (21%)
  local copies, waits for them, and re-layouts  131 us (15%)
  loops' own time  90.6 us (10%)
  starting transfers between devices  88.4 us (10%)
  waiting for transfers between devices  46.4 us (5%)
  between operations  16.1 us (2%)
    unnamed x1, blocking collectives  289 us
    add x127, other arithmetic, chain_combine(): return (earlier_count + later_count, carried + later_error)  128 us
    another operation x1, loops' own time, carried_in(): return lax.fori_loop(0, place, one, state)  83.6 us
    dynamic_slice x127, local copies, waits for them, and re-layouts, one(): lax.dynamic_index_in_dim(a, hop, 0, False)  82.5 us
    ppermute x47, starting transfers between devices, with_halo(): lax.ppermute(lax.slice_in_dim(block, block.shape[dim] - width, None, axis...  72.8 us
    slice x254, local copies, waits for them, and re-layouts, coarse_apply(): jnp.roll(state, -1, 1)  33.3 us
    add x127, other arithmetic, coarse_apply(): coarse_center * state + coarse_behind * jnp.roll(state, 1, 0)  33.2 us
    ppermute x47, waiting for transfers between devices, with_halo(): lax.ppermute(lax.slice_in_dim(block, block.shape[dim] - width, None, axis...  23.4 us
  transfers between devices with their start and end apart: 97, of which 96 were waited for; matrix products, arithmetic and copies ran while one was open for 1% of the time, Pallas kernels for 0%

commit v1 on v0

v1 whole, which is shorter than its diff:
```python
import jax
import jax.numpy as jnp
import numpy as np
from jax import lax
from jax.experimental import pallas as pl
from jax.experimental.pallas import tpu as pltpu
from jax.sharding import PartitionSpec as P

ROWS = 512
HALF = ROWS // 2
COLS = 128
LANES = COLS // 2
STEPS = 16
GROUP = 32
QUAD = 4

fine_center = 0.2
fine_behind = 0.25
fine_ahead = 0.15
coarse_center = 0.04
coarse_behind = 0.31
coarse_ahead = 0.17

HIGHEST = lax.Precision.HIGHEST

GUESS, DEFECT, MEAN_STATE, MEAN_SOURCE, COARSE = 0, 1, 2, 3, 4
LAST = 10
INIT_T, INIT_C = 11, 12
N_OPS = 13


def symbol(theta, phi, center, behind, ahead):
    return (
        center
        + behind * np.exp(-1j * theta)
        + ahead * np.exp(1j * theta)
        + behind * np.exp(-1j * phi)
        + ahead * np.exp(1j * phi)
    )


def operators(theta, phi):
    fine = symbol(theta, phi, fine_center, fine_behind, fine_ahead)
    coarse = symbol(theta, phi, coarse_center, coarse_behind, coarse_ahead)
    power, total = np.ones_like(fine), np.zeros_like(fine)
    inner_sum = np.zeros_like(fine)
    inner_power = np.zeros_like(fine)
    for step in range(STEPS):
        total = total + power
        if step < STEPS - 1:
            inner_sum = inner_sum + total
        power = power * fine
        if step < STEPS - 1:
            inner_power = inner_power + power
    found = [total, power, inner_power / (STEPS - 1), inner_sum / (STEPS - 1)]
    found += [coarse ** (1 << n) for n in range(6)]
    found.append(power * coarse ** (GROUP - 1))
    by_group = []
    for x in range(4):
        from_start = power * coarse ** (GROUP * x - 1) if x else np.ones_like(fine)
        by_group.append(np.stack(found + [coarse ** (GROUP * x), from_start]))
    return np.stack(by_group)


def slice_rows():
    core = np.arange(2)[:, None, None]
    q = np.arange(GROUP)[None, :, None]
    return 2 * (QUAD * q + np.arange(QUAD)[None, None, :]) + core


def mode_table():
    d = slice_rows()[..., None]
    lane = np.arange(COLS)
    row = np.where(lane > LANES, d + HALF, d)
    theta = 2 * np.pi * row / ROWS
    phi = np.where(lane == LANES, np.pi, 2 * np.pi * (lane % LANES) / COLS)
    value = operators(theta, phi + 0 * theta)
    on_u, on_v, across = value.real.copy(), value.real.copy(), value.imag.copy()
    for at, angle in ((0, 0.0), (LANES, np.pi)):
        on_u[:, :, 0, 0, 0, at] = operators(np.array(0.0), np.array(angle)).real
        on_v[:, :, 0, 0, 0, at] = operators(np.array(np.pi), np.array(angle)).real
        across[:, :, 0, 0, 0, at] = 0.0
    table = np.concatenate([on_u, on_v, -across, across], axis=4)
    table = np.moveaxis(table, 1, 3)
    return table.reshape(4, 2, GROUP, 16 * N_OPS, COLS).astype(np.float32)


def row_table():
    turns = slice_rows()[..., None] * np.arange(HALF) % ROWS
    angle = 2 * np.pi * turns / ROWS
    table = np.concatenate([np.cos(angle), np.sin(angle)], axis=2)
    return table.reshape(2, HALF, HALF).astype(np.float32)


def column_tables():
    c = np.arange(COLS)[:, None]
    n = np.arange(LANES)[None, :]
    angle = 2 * np.pi * ((c * n) % COLS) / COLS
    forward = np.concatenate([np.cos(angle), -np.sin(angle)], 1)
    forward[:, LANES] = np.where(np.arange(COLS) % 2 == 0, 1.0, -1.0)
    backward = 2.0 * forward.T / (ROWS * COLS)
    return forward.astype(np.float32), backward.astype(np.float32)


def dot(a, b):
    return jnp.dot(a, b, precision=HIGHEST, preferred_element_type=jnp.float32)


def swap(x):
    return pltpu.roll(x, LANES, x.ndim - 1)


def flip(x):
    return pltpu.roll(x, QUAD, x.ndim - 2)


def tiles(x):
    return x.reshape(x.shape[0] // 8, 8, x.shape[1])


def iota(shape, dim):
    return lax.broadcasted_iota(jnp.int32, shape, dim)


def alternating(shape):
    return (1 - 2 * (iota(shape, 0) % 2)).astype(jnp.float32)


def prepare_kernel(src, init, rows, rows_t, table, src_o, init_o, rows_o, rows_t_o, table_o, sems):
    core = lax.axis_index("sp")
    pairs = (
        (src, src_o),
        (rows.at[core], rows_o),
        (init, init_o),
        (table.at[lax.axis_index("tg"), core, lax.axis_index("tc")], table_o),
        (rows_t.at[core], rows_t_o),
    )
    copies = [pltpu.make_async_copy(a, b, sems.at[n]) for n, (a, b) in enumerate(pairs)]
    for copy in copies:
        copy.start()
    for copy in copies:
        copy.wait()


def to_modes(product, first):
    a, b = tiles(product[:, :COLS]), tiles(product[:, COLS:])
    sub = iota(a.shape, 1)
    lane = iota(a.shape, 2)
    sign = jnp.where(sub < QUAD, 1.0, -1.0)
    own = sign * a
    b_flip = flip(b)
    result = jnp.where(lane < LANES, own + swap(flip(a)), swap(sign * b) + b_flip)
    edge = lane % LANES == 0
    zero_mode = jnp.logical_and(first, jnp.logical_and(iota(a.shape, 0) == 0, sub == QUAD))
    result = jnp.where(edge, jnp.where(zero_mode, b_flip, own), result)
    return result.reshape(product.shape[0], COLS)


def forward_kernel(src, src_other, init, init_other, col, rows, out, init_out):
    core = lax.axis_index("sp")
    own_sign = (1 - 2 * core).astype(jnp.float32)
    sign = alternating((HALF, COLS))

    def columns(own, other):
        y = dot(own_sign * own[...] + other[...], col[...])
        return jnp.concatenate([y, y * sign], axis=1)

    out[...] = to_modes(dot(rows[...], columns(src, src_other)), core == 0)
    at = lax.axis_index("tc")
    own_rows = rows[pl.ds(pl.multiple_of(8 * at, 8), 8), :]
    product = dot(own_rows, columns(init, init_other))
    init_out[...] = to_modes(product, jnp.logical_and(core == 0, at == 0))


class Operators:
    def __init__(self, table):
        self.table = table

    def __call__(self, n, x):
        itself, partner = (self.table[16 * n + j : 16 * n + j + 8] for j in (0, 8))
        return itself * x + partner * flip(x)


def scan_kernel(got, table, c_out, mean_out, message):
    op = Operators(table)
    f = tiles(got[...])
    w = op(GUESS, f)
    t = w
    for level in range(5):
        d = 1 << level
        t = jnp.concatenate([t[:d], t[d:] + op(COARSE + level, t[:-d])], 0)
    c = jnp.concatenate([w[:1], w[1:] + op(DEFECT, t[:-1])], 0)
    source_part = op(MEAN_SOURCE, f)
    mean = jnp.concatenate([source_part[:1], source_part[1:] + op(MEAN_STATE, c[:-1])], 0)
    c_out[...] = c.reshape(HALF, COLS)
    mean_out[...] = mean.reshape(HALF, COLS)
    message[:8] = t[GROUP - 1]
    message[8:] = c[GROUP - 1]


def join_kernel(own, other, table, message, kept):
    op = Operators(table)
    later = lax.axis_index("tg") % 2 == 1
    mine, mine_c, theirs, theirs_c = own[:8], own[8:], other[:8], other[8:]
    prefix = jnp.where(later, theirs, 0.0)
    low = jnp.where(later, theirs, mine)
    high = jnp.where(later, mine, theirs)
    message[:8] = op(COARSE + 5, low) + high
    message[8:] = mine_c + op(LAST, prefix)
    kept[:8] = prefix
    kept[8:] = jnp.where(later, theirs_c, 0.0)


def finish_kernel(c_in, mean_in, kept, other, init, table, out):
    op = Operators(table)
    x = lax.axis_index("tg")
    second = x >= 2
    at_start = x % 2 == 0
    low = jnp.where(second, other[:8], 0.0)
    low_c = jnp.where(second, other[8:], 0.0)
    init_v = init[...]
    carry = kept[:8] + jnp.where(at_start, low, op(COARSE + 5, low)) + op(INIT_T, init_v)
    before = kept[8:] + jnp.where(at_start, low_c, op(LAST, low)) + op(INIT_C, init_v)
    spread = carry[None]
    for level in range(5):
        spread = jnp.concatenate([spread, op(COARSE + level, spread)], 0)
    added = op(DEFECT, spread)
    c = tiles(c_in[...]) + added
    shift = jnp.concatenate([before[None], added[:-1]], 0)
    mean = tiles(mean_in[...]) + op(MEAN_STATE, shift)
    out[:, :8] = c
    out[:, 8:] = mean


def backward_kernel(got, rows_t, col, out, own_out):
    core = lax.axis_index("sp")
    got_v = got[...]
    parts = [got_v[:, :8], got_v[:, 8:]]
    sub = iota(parts[0].shape, 1)
    flat = lambda v: v.reshape(HALF, COLS)
    left = [flat(jnp.where(sub < QUAD, v, -v)) for v in parts]
    right = [flat(flip(v)) for v in parts]
    product = dot(rows_t[...], jnp.concatenate(left + right, axis=1))
    sign = alternating((HALF, COLS))
    lane = iota((HALF, COLS), 1)
    own_sign = (1 - 2 * core).astype(jnp.float32)
    zero_mode = jnp.where(core == 0, 0.5, 0.0)
    for n, v in enumerate(parts):
        e = product[:, COLS * n : COLS * (n + 1)]
        f = product[:, COLS * (n + 2) : COLS * (n + 3)]
        y = jnp.where(lane < LANES, e + sign * swap(e), swap(f) + sign * f)
        first_u, first_v = v[0, :1], v[0, QUAD : QUAD + 1]
        edge = e + zero_mode * (sign * first_v - first_u)
        part = dot(jnp.where(lane % LANES == 0, edge, y), col[...])
        out[n] = part
        own_out[n] = own_sign * part


PARAMS = pltpu.CompilerParams(vmem_limit_bytes=32 * 1024 * 1024)


def call(kernel, shapes, args, hbm=False, scratch=()):
    space = pltpu.HBM if hbm else pltpu.VMEM
    return pl.pallas_call(
        kernel,
        out_shape=[jax.ShapeDtypeStruct(s, jnp.float32) for s in shapes],
        in_specs=[pl.BlockSpec(memory_space=space)] * len(args),
        out_specs=[pl.BlockSpec(memory_space=pltpu.VMEM)] * len(shapes),
        scratch_shapes=scratch,
        compiler_params=PARAMS,
    )(*args)


def shards(initial, source):
    rows = row_table()
    forward, backward = column_tables()
    own = source[0]
    swap_cores = [(0, 1), (1, 0)]
    src_other = lax.ppermute(own, "sp", swap_cores)
    init_other = lax.ppermute(initial, "sp", swap_cores)
    block = (HALF, COLS)
    square = (HALF, HALF)
    src, init, rows_v, rows_t_v, table = call(
        prepare_kernel,
        [block, block, square, square, (16 * N_OPS, COLS)],
        [own, initial, rows, rows.transpose(0, 2, 1).copy(), mode_table()],
        hbm=True,
        scratch=[pltpu.SemaphoreType.DMA((5,))],
    )
    tile, two = (8, COLS), (16, COLS)
    sent, init_modes = call(
        forward_kernel, [block, tile], [src, src_other, init, init_other, forward, rows_v]
    )
    got = lax.all_to_all(sent.reshape(GROUP, 8, COLS), "tc", 0, 0, tiled=True)
    c, mean, message = call(scan_kernel, [block, block, two], [got.reshape(block), table])
    other = lax.ppermute(message, "tg", [(i, i ^ 1) for i in range(4)])
    message, kept = call(join_kernel, [two, two], [message, other, table])
    other = lax.ppermute(message, "tg", [(i, 3 - i) for i in range(4)])
    (back,) = call(
        finish_kernel, [(GROUP, 16, COLS)], [c, mean, kept, other, init_modes, table]
    )
    modes = lax.all_to_all(back, "tc", 0, 0, tiled=True)
    part, own_part = call(
        backward_kernel, [(2, HALF, COLS), (2, HALF, COLS)], [modes, rows_t_v, backward]
    )
    other_part = lax.ppermute(part, "sp", swap_cores)
    return own_part[:1] + other_part[:1], own_part[1:] + other_part[1:]


def solution(mesh):
    in_specs = (P("sp", None), P(("tg", "tc"), "sp", None))
    out_specs = (P(("tg", "tc"), "sp", None), P(("tg", "tc"), "sp", None))
    return jax.shard_map(shards, mesh=mesh, in_specs=in_specs, out_specs=out_specs, check_vma=False)
```

time: 864 us -> 57.9 us (0.07)
  the two profiles are of different devices: /device:TPU:255 before, /device:TPU:1 now
where the time goes in v1:
time: 57.9 us; the launch traced here: 57.6 us
  blocking collectives  32.7 us (56%)
  starting transfers between devices  12.4 us (21%)
  local copies, waits for them, and re-layouts  3.9 us (7%)
  waiting for transfers between devices  3.69 us (6%)
  Pallas kernels  3.55 us (6%)
  other arithmetic  0.74 us (1%)
  between operations  0.69 us (1%)
    all_to_all x1, blocking collectives, shards(): got = lax.all_to_all(sent.reshape(GROUP, 8, COLS), 'tc', 0, 0, tiled=True)  18.6 us
    all_to_all x1, blocking collectives, shards(): modes = lax.all_to_all(back, 'tc', 0, 0, tiled=True)  14.1 us
    ppermute x1, starting transfers between devices, shards(): other_part = lax.ppermute(part, 'sp', swap_cores)  5.17 us
    unnamed x12, local copies, waits for them, and re-layouts  3.9 us
    pallas_call x6, Pallas kernels, call(): pl.pallas_call(kernel, out_shape=[jax.ShapeDtypeStruct(s, jnp.float32) fo...  3.55 us
    ppermute x1, starting transfers between devices, shards(): src_other = lax.ppermute(own, 'sp', swap_cores)  3.33 us
    ppermute x1, starting transfers between devices, shards(): other = lax.ppermute(message, 'tg', [(i, 3 - i) for i in range(4)])  2.48 us
    ppermute x1, starting transfers between devices, shards(): other = lax.ppermute(message, 'tg', [(i, i ^ 1) for i in range(4)])  1.3 us
  transfers between devices with their start and end apart: 5, of which 3 were waited for; matrix products, arithmetic and copies ran while one was open for 0% of the time, Pallas kernels for 2%

profile of v1, /device:TPU:1, one launch (start us, length us, event | category | flops | bytes accessed | tf_op | source)
XLA Modules:
  0.0 57.6 jit_solution(7949432700601628144)
XLA Ops:
  0.6 3.3 %collective-permute-start = (f32[256,128]{1,0:T(8,128)}, f32[256,128]{1,0:T(8,128)S(1)}, u32[]{:S(2)}, u32[]{:S(2)}) collective-permute-start(f32[256,128]{1,0:T(8,128)} %bitcast.4), channel_id=1, source_target_pairs={{0,1},{1,0},{2,3},{3,2},{4,5},{5,4},{6,7},{7,6},{8,9},{9,8},{10,11... | collective-permute-start | bytes 393224 | tf_op jit(solution)/shard_map/ppermute | solution.py:279
  4.0 0.1 collective-permute-start.1
  4.1 0.0 copy-start
  4.1 1.0 %copy-done = f32[2,256,256]{2,1,0:T(8,128)S(1)} copy-done((f32[2,256,256]{2,1,0:T(8,128)S(1)}, f32[2,256,256]{2,1,0:T(8,128)}, u32[]{:S(2)}) %copy-start) | copy-done | bytes 524312
  5.1 0.0 copy-start.1
  5.1 1.0 %copy-done.1 = f32[2,256,256]{2,1,0:T(8,128)S(1)} copy-done((f32[2,256,256]{2,1,0:T(8,128)S(1)}, f32[2,256,256]{2,1,0:T(8,128)}, u32[]{:S(2)}) %copy-start.1) | copy-done | bytes 524312
  6.1 0.0 copy-start.2
  6.1 0.9 %copy-done.2 = f32[1,256,128]{2,1,0:T(8,128)S(1)} copy-done((f32[1,256,128]{2,1,0:T(8,128)S(1)}, f32[1,256,128]{2,1,0:T(8,128)}, u32[]{:S(2)}) %copy-start.2) | copy-done | bytes 131096
  7.0 0.0 copy-start.3
  7.0 0.9 %copy-done.3 = f32[256,128]{1,0:T(8,128)S(1)} copy-done((f32[256,128]{1,0:T(8,128)S(1)}, f32[256,128]{1,0:T(8,128)}, u32[]{:S(2)}) %copy-start.3) | copy-done | bytes 131096
  8.0 0.0 copy-start.5
  8.0 0.0 copy-start.4
  8.0 1.3 %shard_map.86 = (f32[256,128]{1,0:T(8,128)S(1)}, f32[256,128]{1,0:T(8,128)S(1)}, f32[256,256]{1,0:T(8,128)S(1)}, f32[256,256]{1,0:T(8,128)S(1)}, f32[208,128]{1,0:T(8,128)S(1)}) custom-call(f32[256,128]{1,0:T(8,128)S(1)} %bitcast.5, f32[256,128]{1,0:T(8,128)S(1)} %copy-done.3, f32[2,256,256]{2,1,0:T(8,128)S(1)} %copy-done.1, f32[2,256,256]{2,1,0:T(8,128)S(1)} %copy-done, ...), custom_call_target="tpu_custom_call" | custom-call | tf_op jit(solution)/shard_map/pallas_call | solution.py:264
  9.2 0.0 collective-permute-done.src_other
  9.3 0.0 collective-permute-done.1.init_other
  9.3 0.0 copy-done.5
  9.3 0.9 %shard_map.87 = (f32[256,128]{1,0:T(8,128)S(1)}, f32[8,128]{1,0:T(8,128)S(1)}) custom-call(f32[256,128]{1,0:T(8,128)S(1)} %get-tuple-element.16.src, f32[256,128]{1,0:T(8,128)S(1)} %collective-permute-done.src_other, f32[256,128]{1,0:T(8,128)S(1)} %get-tuple-element.17.init, f32[256,128]{1,0:T(8,128)S(1)} %collective-permute-done.1.init_other, ...), custom_call_target="tpu_custom_call" | custom-call | tf_op jit(solution)/shard_map/pallas_call | solution.py:264
  10.2 18.6 %all_to_all.10 = f32[32,8,128]{2,1,0:T(8,128)S(1)} all-to-all(f32[32,8,128]{2,1,0:T(8,128)S(1)} %bitcast.6), channel_id=1, replica_groups=mesh['tg'=4,'tc'=32,'sp'=2] {'tc'}, dimensions={0} | all-to-all | bytes 262144 | tf_op jit(solution)/shard_map/all_to_all | solution.py:294
  28.8 0.2 shard_map.88
  29.0 1.3 %collective-permute-start.2 = (f32[16,128]{1,0:T(8,128)S(1)}, f32[16,128]{1,0:T(8,128)S(1)}, u32[]{:S(2)}, u32[]{:S(2)}) collective-permute-start(f32[16,128]{1,0:T(8,128)S(1)} %get-tuple-element.23.own), channel_id=1, source_target_pairs={{0,64},{64,0},{128,192},{192,128},{1,65},{65,1},{129,193},{193,129... | collective-permute-start | bytes 24584 | tf_op jit(solution)/shard_map/ppermute | solution.py:296
  30.3 1.3 %collective-permute-done.2.other = f32[16,128]{1,0:T(8,128)S(1)} collective-permute-done((f32[16,128]{1,0:T(8,128)S(1)}, f32[16,128]{1,0:T(8,128)S(1)}, u32[]{:S(2)}, u32[]{:S(2)}) %collective-permute-start.2) | collective-permute-done | bytes 8224 | tf_op jit(solution)/shard_map/ppermute | solution.py:296
  31.6 2.5 %collective-permute-start.3 = (f32[16,128]{1,0:T(8,128)S(1)}, f32[16,128]{1,0:T(8,128)S(1)}, u32[]{:S(2)}, u32[]{:S(2)}) collective-permute-start(f32[16,128]{1,0:T(8,128)S(1)} %get-tuple-element.25), channel_id=1, source_target_pairs={{0,192},{64,128},{128,64},{192,0},{1,193},{65,129},{129,65},{193,1... | collective-permute-start | bytes 24584 | tf_op jit(solution)/shard_map/ppermute | solution.py:298
  34.1 1.2 %collective-permute-done.3.other = f32[16,128]{1,0:T(8,128)S(1)} collective-permute-done((f32[16,128]{1,0:T(8,128)S(1)}, f32[16,128]{1,0:T(8,128)S(1)}, u32[]{:S(2)}, u32[]{:S(2)}) %collective-permute-start.3) | collective-permute-done | bytes 8224 | tf_op jit(solution)/shard_map/ppermute | solution.py:298
  35.3 0.1 shard_map.90
  35.4 14.1 %all_to_all.11.got = f32[32,16,128]{2,1,0:T(8,128)S(1)} all-to-all(f32[32,16,128]{2,1,0:T(8,128)S(1)} %shard_map.90), channel_id=1, replica_groups=mesh['tg'=4,'tc'=32,'sp'=2] {'tc'}, dimensions={0} | all-to-all | bytes 524288 | tf_op jit(solution)/shard_map/all_to_all | solution.py:302
  49.4 0.0 copy-done.4
  49.5 1.1 %shard_map.91 = (f32[2,256,128]{2,1,0:T(8,128)S(1)}, f32[2,256,128]{2,1,0:T(8,128)S(1)}) custom-call(f32[32,16,128]{2,1,0:T(8,128)S(1)} %all_to_all.11.got, f32[256,256]{1,0:T(8,128)S(1)} %get-tuple-element.27.rows_t, f32[128,128]{1,0:T(8,128)S(1)} %copy-done.4), custom_call_target="tpu_custom_call" | custom-call | tf_op jit(solution)/shard_map/pallas_call | solution.py:264
  50.5 5.2 %collective-permute-start.4 = (f32[2,256,128]{2,1,0:T(8,128)S(1)}, f32[2,256,128]{2,1,0:T(8,128)S(1)}, u32[]{:S(2)}, u32[]{:S(2)}) collective-permute-start(f32[2,256,128]{2,1,0:T(8,128)S(1)} %get-tuple-element.29), channel_id=1, source_target_pairs={{0,1},{1,0},{2,3},{3,2},{4,5},{5,4},{6,7},{7,6},{8,9},{9,8},{10,11... | collective-permute-start | bytes 786440 | tf_op jit(solution)/shard_map/ppermute | solution.py:306
  55.7 1.2 %collective-permute-done.4 = f32[2,256,128]{2,1,0:T(8,128)S(1)} collective-permute-done((f32[2,256,128]{2,1,0:T(8,128)S(1)}, f32[2,256,128]{2,1,0:T(8,128)S(1)}, u32[]{:S(2)}, u32[]{:S(2)}) %collective-permute-start.4) | collective-permute-done | bytes 262176 | tf_op jit(solution)/shard_map/ppermute | solution.py:306
  56.9 0.7 %slice_add_fusion = (f32[1,256,128]{2,1,0:T(8,128)}, f32[1,256,128]{2,1,0:T(8,128)}) fusion(f32[2,256,128]{2,1,0:T(8,128)S(1)} %collective-permute-done.4, f32[2,256,128]{2,1,0:T(8,128)S(1)} %get-tuple-element.28), kind=kLoop, calls=%fused_computation | loop fusion | flops 65536 | bytes 786432 | tf_op jit(solution)/shard_map/add | solution.py:307
  (1 shorter events, 0.0 us)
Async XLA Ops:
  0.6 8.6 %collective-permute-start = (f32[256,128]{1,0:T(8,128)}, f32[256,128]{1,0:T(8,128)S(1)}, u32[]{:S(2)}, u32[]{:S(2)}) collective-permute-start(f32[256,128]{1,0:T(8,128)} %bitcast.4), channel_id=1, source_target_pairs={{0,1},{1,0},{2,3},{3,2},{4,5},{5,4},{6,7},{7,6},{8,9},{9,8},{10,11... | collective-permute-start | bytes 393224 | tf_op jit(solution)/shard_map/ppermute | solution.py:279
  4.0 5.3 %collective-permute-start.1 = (f32[256,128]{1,0:T(8,128)}, f32[256,128]{1,0:T(8,128)S(1)}, u32[]{:S(2)}, u32[]{:S(2)}) collective-permute-start(f32[256,128]{1,0:T(8,128)} %init.1), channel_id=1, source_target_pairs={{0,1},{1,0},{2,3},{3,2},{4,5},{5,4},{6,7},{7,6},{8,9},{9,8},{10,11... | collective-permute-start | bytes 393224 | tf_op jit(solution)/shard_map/ppermute | solution.py:280
  4.1 1.0 %copy-start = (f32[2,256,256]{2,1,0:T(8,128)S(1)}, f32[2,256,256]{2,1,0:T(8,128)}, u32[]{:S(2)}) copy-start(f32[2,256,256]{2,1,0:T(8,128)} %constant.11.clone.rows_t) | copy-start | bytes 1572868
  5.1 1.0 %copy-start.1 = (f32[2,256,256]{2,1,0:T(8,128)S(1)}, f32[2,256,256]{2,1,0:T(8,128)}, u32[]{:S(2)}) copy-start(f32[2,256,256]{2,1,0:T(8,128)} %constant.10.clone.rows) | copy-start | bytes 1572868
  6.1 0.9 %copy-start.2 = (f32[1,256,128]{2,1,0:T(8,128)S(1)}, f32[1,256,128]{2,1,0:T(8,128)}, u32[]{:S(2)}) copy-start(f32[1,256,128]{2,1,0:T(8,128)} %param.8) | copy-start | bytes 393220
  7.0 0.9 %copy-start.3 = (f32[256,128]{1,0:T(8,128)S(1)}, f32[256,128]{1,0:T(8,128)}, u32[]{:S(2)}) copy-start(f32[256,128]{1,0:T(8,128)} %init.1) | copy-start | bytes 393220
  8.0 1.3 %copy-start.5 = (f32[128,128]{1,0:T(8,128)S(1)}, f32[128,128]{1,0:T(8,128)}, u32[]{:S(2)}) copy-start(f32[128,128]{1,0:T(8,128)} %constant.13.clone.col) | copy-start | bytes 196612
  8.0 41.5 %copy-start.4 = (f32[128,128]{1,0:T(8,128)S(1)}, f32[128,128]{1,0:T(8,128)}, u32[]{:S(2)}) copy-start(f32[128,128]{1,0:T(8,128)} %constant.14.clone.col) | copy-start | bytes 196612
  29.0 2.6 %collective-permute-start.2 = (f32[16,128]{1,0:T(8,128)S(1)}, f32[16,128]{1,0:T(8,128)S(1)}, u32[]{:S(2)}, u32[]{:S(2)}) collective-permute-start(f32[16,128]{1,0:T(8,128)S(1)} %get-tuple-element.23.own), channel_id=1, source_target_pairs={{0,64},{64,0},{128,192},{192,128},{1,65},{65,1},{129,193},{193,129... | collective-permute-start | bytes 24584 | tf_op jit(solution)/shard_map/ppermute | solution.py:296
  31.6 3.7 %collective-permute-start.3 = (f32[16,128]{1,0:T(8,128)S(1)}, f32[16,128]{1,0:T(8,128)S(1)}, u32[]{:S(2)}, u32[]{:S(2)}) collective-permute-start(f32[16,128]{1,0:T(8,128)S(1)} %get-tuple-element.25), channel_id=1, source_target_pairs={{0,192},{64,128},{128,64},{192,0},{1,193},{65,129},{129,65},{193,1... | collective-permute-start | bytes 24584 | tf_op jit(solution)/shard_map/ppermute | solution.py:298
  50.5 6.3 %collective-permute-start.4 = (f32[2,256,128]{2,1,0:T(8,128)S(1)}, f32[2,256,128]{2,1,0:T(8,128)S(1)}, u32[]{:S(2)}, u32[]{:S(2)}) collective-permute-start(f32[2,256,128]{2,1,0:T(8,128)S(1)} %get-tuple-element.29), channel_id=1, source_target_pairs={{0,1},{1,0},{2,3},{3,2},{4,5},{5,4},{6,7},{7,6},{8,9},{9,8},{10,11... | collective-permute-start | bytes 786440 | tf_op jit(solution)/shard_map/ppermute | solution.py:306
